TPU v7x, 32 devices: a whole 2x2x4 slice. The times are simulated.
32 devices in a mesh: section: 4 (over y, x), expert: 8 (over z, core).
Axes of the slice: x: 2, y: 2, z: 4, core: 2. Of those that a mesh axis runs over, the one named last changes fastest.
Arguments:
- tokens: bfloat16 [4096, 4096], P(('section', 'expert')), may hold values from -6 to 6
- expert_ids: int32 [4096], P(('section', 'expert')), may hold values from 0 to 7, as said below
- slot_ids: int32 [4096], P(('section', 'expert')), may hold values from 0 to 19, as said below
- router: bfloat16 [4096, 8], replicated, may hold values from -0.09375 to 0.09375
- w_in: bfloat16 [8, 4096, 5120], P('expert', None, 'section'), may hold values from -0.09375 to 0.09375
- w_out: bfloat16 [8, 5120, 4096], P('expert', 'section'), may hold values from -0.078125 to 0.078125
Outputs:
- moe_out: bfloat16 [4096, 4096], P(('section', 'expert'))
Inputs may be any that keep to these rules, and one draw needn't show every extreme that they name: `expert_ids`: within each aligned block of 128 rows (the tokens of one device) no pair of expert id and slot position occurs twice, so each expert receives at most 20 tokens from one device. `slot_ids`: a token's position among the 20 slots that its device keeps for its expert.
All inputs are finite; a program needn't handle non-finite values.
Results may differ from a plain program's by a relative error of at most 0.018.
Values may be sent and summed in bfloat16 or wider, within the bound.
A program may use at most 128 MiB of HBM per device.

v0:
```python
import jax
import jax.numpy as jnp
from jax import lax
from jax.sharding import PartitionSpec as P


def per_device(tokens, expert_ids, slot_ids, router, w_in, w_out):
    tok_rows, width_model = tokens.shape
    experts = router.shape[1]
    capacity = 5 * tok_rows // (4 * experts)
    cell_index = expert_ids * capacity + slot_ids
    onehot = (
        cell_index[None, :] == jnp.arange(experts * capacity, dtype=jnp.int32)[:, None]
    ).astype(jnp.bfloat16)
    dispatch = jnp.dot(onehot, tokens, preferred_element_type=jnp.float32).astype(jnp.bfloat16)
    dispatch = dispatch.reshape(1, experts, capacity, width_model)
    inward = w_in[0]
    outward = w_out[0]
    grouped = lax.all_gather(dispatch, "section", axis=0, tiled=True)
    arrived = lax.all_to_all(grouped, "expert", split_axis=1, concat_axis=1, tiled=True)
    flat = arrived.reshape(-1, width_model)
    hidden = jax.nn.relu(jnp.dot(flat, inward, preferred_element_type=jnp.float32)).astype(
        jnp.bfloat16
    )
    summed = lax.psum_scatter(
        jnp.dot(hidden, outward, preferred_element_type=jnp.float32).astype(jnp.bfloat16),
        "section",
        scatter_dimension=0,
        tiled=True,
    )
    expert_out = summed.reshape(experts, capacity, width_model)
    returned = lax.all_to_all(expert_out, "expert", split_axis=0, concat_axis=0, tiled=True)
    combined = lax.dot_general(
        onehot,
        returned.reshape(-1, width_model),
        (((0,), (0,)), ((), ())),
        preferred_element_type=jnp.float32,
    )
    logits = jnp.dot(tokens, router, preferred_element_type=jnp.float32)
    chosen = expert_ids[:, None] == jnp.arange(experts, dtype=jnp.int32)[None, :]
    gating = jax.nn.sigmoid(jnp.sum(jnp.where(chosen, logits, jnp.zeros_like(logits)), axis=1))
    return (gating[:, None] * combined).astype(jnp.bfloat16)


def solution(mesh):
    return jax.shard_map(
        per_device,
        mesh=mesh,
        in_specs=(
            P(("section", "expert"), None),
            P(("section", "expert")),
            P(("section", "expert")),
            P(),
            P("expert", None, "section"),
            P("expert", "section", None),
        ),
        out_specs=P(("section", "expert"), None),
        check_vma=False,
    )
```

profile of v0, /device:TPU:0, one launch (start us, length us, event | category | flops | bytes accessed | tf_op | source)
XLA Modules:
  0.0 359.0 jit_solution(13831922622663773395)
XLA Ops:
  6.5 0.0 copy-start
  6.5 0.0 all-gather.2.cloned.1.call-start
  6.5 0.8 multiply_add_fusion
  7.3 0.0 copy-start.2
  7.3 0.5 copy-done.2
  7.8 0.0 copy-done
  7.8 1.6 convolution_convert_fusion
  9.4 1.4 reshape.20
  10.8 1.8 copy.7
  12.7 0.0 all-gather.2.cloned.1.call-update
  12.7 0.0 reduce-scatter.2.cloned.1.call-start
  12.7 64.2 %all-gather.2.cloned.1.call-done = bf16[4,8,20,4096]{3,1,2,0:T(8,128)(2,1)} async-done(((bf16[1,8,20,4096]{3,1,2,0:T(8,128)(2,1)}), bf16[4,8,20,4096]{3,1,2,0:T(8,128)(2,1)}) %all-gather.2.cloned.1.call-update) | async-done | bytes 5242896 | tf_op jit(solution)/shard_map/all_gather | solution.py:19
  77.0 6.5 %copy.8 = bf16[4,8,20,4096]{3,0,2,1:T(4,128)(2,1)S(1)} copy(bf16[4,8,20,4096]{3,1,2,0:T(8,128)(2,1)} %all-gather.2.cloned.1.call-done) | data formatting | bytes 10485760 | tf_op jit(solution)/shard_map/all_gather | solution.py:19
  83.5 121.0 %all_to_all.10 = bf16[4,8,20,4096]{3,0,2,1:T(4,128)(2,1)S(1)} all-to-all(bf16[4,8,20,4096]{3,0,2,1:T(4,128)(2,1)S(1)} %copy.8), channel_id=1, replica_groups=mesh['section'=4,'expert'=8] {'expert'}, dimensions={1} | all-to-all | bytes 10485760 | tf_op jit(solution)/shard_map/all_to_all | solution.py:20
  204.5 5.6 %copy.9 = bf16[4,8,20,4096]{3,2,1,0:T(8,128)(2,1)} copy(bf16[4,8,20,4096]{3,0,2,1:T(4,128)(2,1)S(1)} %all_to_all.10) | data formatting | bytes 10485760 | tf_op jit(solution)/shard_map/all_to_all | solution.py:20
  210.1 7.8 %reshape.21 = bf16[640,4096]{1,0:T(8,128)(2,1)} reshape(bf16[4,8,20,4096]{3,2,1,0:T(8,128)(2,1)} %copy.9) | data formatting | bytes 10485760 | tf_op jit(solution)/shard_map/reshape | solution.py:21
  217.9 25.9 %fusion.4 = bf16[640,4096]{1,0:T(8,128)(2,1)} fusion(bf16[1,1280,4096]{2,1,0:T(8,128)(2,1)} %param.11, bf16[640,4096]{1,0:T(8,128)(2,1)} %reshape.21, bf16[1,4096,1280]{2,1,0:T(8,128)(2,1)} %param.10), kind=kOutput, calls=%fused_computation.4 | convolution fusion | flops 13426032640 | bytes 31457280 | tf_op jit(solution)/shard_map/dot_general | solution.py:26
  243.9 0.0 copy-start.1
  243.9 0.0 copy-start.4
  243.9 0.0 reduce-scatter.2.cloned.1.call-update
  243.9 0.0 copy-start.3
  243.9 59.4 %reduce-scatter.2.cloned.1.call-done = bf16[160,4096]{1,0:T(8,128)(2,1)} async-done(((bf16[640,4096]{1,0:T(8,128)(2,1)}), bf16[160,4096]{1,0:T(8,128)(2,1)}) %reduce-scatter.2.cloned.1.call-update) | async-done | bytes 1310736 | tf_op jit(solution)/shard_map/reduce_scatter | solution.py:25
  303.3 2.4 reshape.22
  305.7 4.6 %all-to-all-start.1 = ((bf16[8,20,4096]{2,1,0:T(8,128)(2,1)}), bf16[8,20,4096]{2,1,0:T(8,128)(2,1)S(1)}, u32[]{:S(2)}, u32[]{:S(2)}) async-start(bf16[8,20,4096]{2,1,0:T(8,128)(2,1)} %reshape.22), calls=%async_computation.2 | async-start | bytes 3145728 | tf_op jit(solution)/shard_map/all_to_all | solution.py:32
  310.3 0.0 copy-done.1
  310.3 0.0 copy-done.4
  310.3 0.4 fusion.17
  310.7 37.4 %all-to-all-done.1 = bf16[8,20,4096]{2,1,0:T(8,128)(2,1)S(1)} async-done(((bf16[8,20,4096]{2,1,0:T(8,128)(2,1)}), bf16[8,20,4096]{2,1,0:T(8,128)(2,1)S(1)}, u32[]{:S(2)}, u32[]{:S(2)}) %all-to-all-start.1) | async-done | bytes 1310752 | tf_op jit(solution)/shard_map/all_to_all | solution.py:32
  348.1 1.2 reshape.23
  349.3 0.0 copy-done.3
  349.3 2.8 fusion.7
  (1 shorter events, 0.0 us)
Async XLA Ops:
  6.5 1.3 copy-start
  6.5 70.4 %all-gather.2.cloned.1.call-start = ((), (), s32[]{:S(2)}) async-start(), calls=%async_computation.3 | async-start | bytes 6553600 | tf_op jit(solution)/shard_map/all_gather | solution.py:19
  7.3 0.5 copy-start.2
  12.7 290.6 %reduce-scatter.2.cloned.1.call-start = ((), (), s32[]{:S(2)}) async-start(), calls=%async_computation.4 | async-start | bytes 6553600 | tf_op jit(solution)/shard_map/reduce_scatter | solution.py:25
  243.9 66.4 %copy-start.1 = (bf16[4096,8]{0,1:T(8,128)(2,1)S(1)}, bf16[4096,8]{0,1:T(8,128)(2,1)}, u32[]{:S(2)}) copy-start(bf16[4096,8]{0,1:T(8,128)(2,1)} %param.9) | copy-start | bytes 196612
  243.9 66.4 %copy-start.4 = (s32[128]{0:T(128)S(1)}, s32[128]{0:T(128)}, u32[]{:S(2)}) copy-start(s32[128]{0:T(128)} %param.7) | copy-start | bytes 1540
  243.9 105.5 %copy-start.3 = (s32[128]{0:T(128)S(1)}, s32[128]{0:T(128)}, u32[]{:S(2)}) copy-start(s32[128]{0:T(128)} %copy-done.2) | copy-start | bytes 1540
  305.7 42.4 %all-to-all-start.1 = ((bf16[8,20,4096]{2,1,0:T(8,128)(2,1)}), bf16[8,20,4096]{2,1,0:T(8,128)(2,1)S(1)}, u32[]{:S(2)}, u32[]{:S(2)}) async-start(bf16[8,20,4096]{2,1,0:T(8,128)(2,1)} %reshape.22), calls=%async_computation.2 | async-start | bytes 3145728 | tf_op jit(solution)/shard_map/all_to_all | solution.py:32
Sparse Core Ops, SparseCore 0:
  12.8 64.1 all-gather.1
  244.0 59.2 reduce-scatter.1
where the time goes:
time: 359 us
  waiting for transfers between devices  161 us (45%)
  blocking collectives  121 us (34%)
  matrix products  30.7 us (9%)
  local copies, waits for them, and re-layouts  27.3 us (8%)
  between operations  13.4 us (4%)
  starting transfers between devices  4.64 us (1%)
    all_to_all x1, blocking collectives, per_device(): lax.all_to_all(grouped, 'expert', split_axis=1, concat_axis=1, tiled=True)  121 us
    all_gather x1, waiting for transfers between devices, per_device(): grouped = lax.all_gather(dispatch, 'section', axis=0, tiled=True)  64.2 us
    reduce_scatter x1, waiting for transfers between devices, per_device(): lax.psum_scatter(jnp.dot(hidden, outward, preferred_element_type=jnp.floa...  59.4 us
    all_to_all x1, waiting for transfers between devices, per_device(): lax.all_to_all(expert_out, 'expert', split_axis=0, concat_axis=0, tiled=T...  37.4 us
    dot_general x1, matrix products, per_device(): jnp.dot(hidden, outward, preferred_element_type=jnp.float32)  25.9 us
    reshape x1, local copies, waits for them, and re-layouts, per_device(): flat = arrived.reshape(-1, width_model)  7.83 us
  transfers between devices with their start and end apart: 3, of which 3 were waited for; matrix products, arithmetic and copies ran while one was open for 0% of the time, Pallas kernels for 0%

commit v1 on v0

--- a/solution.py
+++ b/solution.py
@@ -1,7 +1,17 @@
+import functools
+import math
+
 import jax
 import jax.numpy as jnp
 from jax import lax
+from jax.experimental import pallas as pl
+from jax.experimental.pallas import tpu as pltpu
 from jax.sharding import PartitionSpec as P
+
+MESH = pl.DeviceIdType.MESH
+BF16 = jnp.bfloat16
+F32 = jnp.float32
+CHUNKS = 8
 
 
 def per_device(tokens, expert_ids, slot_ids, router, w_in, w_out):
@@ -13,12 +23,11 @@
         cell_index[None, :] == jnp.arange(experts * capacity, dtype=jnp.int32)[:, None]
     ).astype(jnp.bfloat16)
     dispatch = jnp.dot(onehot, tokens, preferred_element_type=jnp.float32).astype(jnp.bfloat16)
-    dispatch = dispatch.reshape(1, experts, capacity, width_model)
+    dispatch = dispatch.reshape(experts, capacity, width_model)
     inward = w_in[0]
     outward = w_out[0]
-    grouped = lax.all_gather(dispatch, "section", axis=0, tiled=True)
-    arrived = lax.all_to_all(grouped, "expert", split_axis=1, concat_axis=1, tiled=True)
-    flat = arrived.reshape(-1, width_model)
+    arrived = lax.all_to_all(dispatch, "expert", split_axis=0, concat_axis=0, tiled=True)
+    flat = lax.all_gather(arrived.reshape(-1, width_model), "section", axis=0, tiled=True)
     hidden = jax.nn.relu(jnp.dot(flat, inward, preferred_element_type=jnp.float32)).astype(
         jnp.bfloat16
     )
@@ -42,9 +51,310 @@
     return (gating[:, None] * combined).astype(jnp.bfloat16)
 
 
+def divide(value, number):
+    return lax.shift_right_logical(value * (-(-(1 << 20) // number)), 20)
+
+
+def iota(shape, dim):
+    return lax.broadcasted_iota(jnp.int32, shape, dim)
+
+
+def one_where(condition):
+    return jnp.where(condition, 1.0, 0.0).astype(BF16)
+
+
+def dot(a, b):
+    return jnp.dot(a, b, preferred_element_type=F32)
+
+
+def kernel(
+    dims, tok, eid, sid, router, w_in, w_out, out,
+    disp, arr, xall, acc, hid, win, wout, part, half, fin, back, ret,
+    d_mat, p_mat, pt_mat, c_mat, gate,
+    win_sem, wout_sem, d_send, d_recv, g_send, g_recv, s_send, s_recv, b_send, b_recv,
+):
+    E, C, Q, G, W, S, T, H = dims
+    B, R = Q * C, E * C
+    h = R // 2
+    section, expert = lax.axis_index("section"), lax.axis_index("expert")
+    y, x = section // 2, section % 2
+    xn = {"section": y * 2 + (1 - x), "expert": expert}
+    yn = {"section": (1 - y) * 2 + x, "expert": expert}
+    peers = [(expert + d) % E for d in range(1, E)]
+
+    def in_copy(c):
+        return pltpu.make_async_copy(w_in.at[0, pl.ds(c * W, W)], win.at[c], win_sem.at[c])
+
+    def out_copy(c):
+        columns = pl.ds(pl.multiple_of(c * W, W), W)
+        return pltpu.make_async_copy(w_out.at[0, :, columns], wout.at[c], wout_sem.at[c])
+
+    def exchange_start(src, dst, send, recv, c):
+        mine = pl.ds(expert * B, B)
+        for p in peers:
+            pltpu.make_async_remote_copy(
+                src_ref=src.at[c, pl.ds(p * B, B)],
+                dst_ref=dst.at[c, mine],
+                send_sem=send.at[c],
+                recv_sem=recv.at[c],
+                device_id={"section": section, "expert": p},
+                device_id_type=MESH,
+            ).start()
+        pltpu.make_async_copy(src.at[c, mine], dst.at[c, mine], recv.at[c]).start()
+
+    def exchange_arrived(dst, recv, c):
+        pltpu.make_async_copy(dst.at[c], dst.at[c], recv.at[c]).wait()
+
+    def exchange_sent(src, send, c):
+        others = src.at[c, pl.ds(0, (E - 1) * B)]
+        pltpu.make_async_copy(others, others, send.at[c]).wait()
+
+    def hop(src, src_row, dst, dst_row, rows, send, recv, index, c, target):
+        return pltpu.make_async_remote_copy(
+            src_ref=src.at[c, pl.ds(src_row, rows)],
+            dst_ref=dst.at[c, pl.ds(dst_row, rows)],
+            send_sem=send.at[index, c],
+            recv_sem=recv.at[index, c],
+            device_id=target,
+            device_id_type=MESH,
+        )
+
+    def gather_hop(index, c):
+        src_row, dst_row, rows, target = (
+            (0, R, R, xn),
+            (0, 2 * R, R, yn),
+            (R, 3 * R, h, yn),
+            (2 * R + h, 3 * R + h, h, xn),
+        )[index]
+        return hop(xall, src_row, xall, dst_row, rows, g_send, g_recv, index, c, target)
+
+    def scatter_hop(index, c):
+        src_row, dst, dst_row, target = (
+            (3 * R, half, 0, xn),
+            (3 * R + h, half, h, yn),
+            (R, fin, 0, xn),
+            (2 * R + h, fin, R + h, yn),
+            (R + h, fin, h, xn),
+            (2 * R, fin, R, yn),
+        )[index]
+        return hop(part, src_row, dst, dst_row, h, s_send, s_recv, index, c, target)
+
+    barrier = pltpu.get_barrier_semaphore()
+    for p in peers:
+        pl.semaphore_signal(
+            barrier, inc=1, device_id={"section": section, "expert": p}, device_id_type=MESH
+        )
+    for target in (xn, yn):
+        pl.semaphore_signal(barrier, inc=1, device_id=target, device_id_type=MESH)
+
+    def keys(shape, dim):
+        r = iota(shape, dim)
+        block = divide(r, B)
+        inner = r - block * B
+        quarter = divide(inner, C)
+        return quarter * R + block * C + (inner - quarter * C)
+
+    cell_row = eid[...] * C + sid[...]
+    diagonal = iota((T, T), 0) == iota((T, T), 1)
+    column = lambda row: jnp.sum(
+        jnp.where(diagonal, jnp.broadcast_to(row, (T, T)), 0).astype(F32), axis=1, keepdims=True
+    ).astype(jnp.int32)
+
+    key = keys((E * B, T), 0)
+    for q in range(Q):
+        d_mat[q] = one_where(key == cell_row + q * R)
+
+    def dispatch(c):
+        total = None
+        for q in range(Q):
+            columns = pl.ds(pl.multiple_of(c * W + q * S, S), S)
+            term = dot(d_mat[q], tok[:, columns])
+            total = term if total is None else total + term
+        disp[c] = total.astype(BF16)
+
+    dispatch(0)
+    pl.semaphore_wait(barrier, E + 1)
+    exchange_start(disp, arr, d_send, d_recv, 0)
+
+    @pl.loop(0, G)
+    def _(c):
+        in_copy(c).start()
+
+    key = keys((R, E * B), 1)
+    for q in range(Q):
+        p_mat[q] = one_where(key == iota((R, E * B), 0) + q * R)
+
+    @pl.loop(0, G + 2)
+    def _(c):
+        @pl.when(c + 1 < G)
+        def _():
+            dispatch(c + 1)
+            exchange_start(disp, arr, d_send, d_recv, c + 1)
+
+        @pl.when(c < G)
+        def _():
+            out_copy(c).start()
+            exchange_arrived(arr, d_recv, c)
+            for q in range(Q):
+                xall[c, 0:R, q * S : (q + 1) * S] = dot(p_mat[q], arr[c]).astype(BF16)
+            gather_hop(0, c).start()
+            gather_hop(1, c).start()
+
+        @pl.when(c == 0)
+        def _():
+            key = keys((E * B, R), 0)
+            for q in range(Q):
+                pt_mat[q] = one_where(key == iota((E * B, R), 1) + q * R)
+            key = keys((T, E * B), 1)
+            cell_column = column(cell_row)
+            for q in range(Q):
+                c_mat[q] = one_where(key == cell_column + q * R)
+            logits = dot(tok[...], router[...])
+            chosen = column(eid[...]) == iota((T, E), 1)
+            picked = jnp.sum(jnp.where(chosen, logits, 0.0), axis=1, keepdims=True)
+            gate[...] = 1.0 / (1.0 + jnp.exp(-picked))
+            acc[...] = jnp.zeros_like(acc)
+
+        @pl.when((c >= 1) & (c <= G))
+        def _():
+            k = c - 1
+            gather_hop(0, k).wait_recv()
+            gather_hop(2, k).start()
+            gather_hop(1, k).wait_recv()
+            gather_hop(3, k).start()
+
+        @pl.when(c >= 2)
+        def _():
+            k = c - 2
+            gather_hop(2, k).wait_recv()
+            gather_hop(3, k).wait_recv()
+            in_copy(k).wait()
+
+            @pl.loop(0, H // 256)
+            def _(n):
+                columns = pl.ds(pl.multiple_of(n * 256, 256), 256)
+                acc[:, columns] += dot(xall[k], win[k, :, columns])
+
+    @pl.loop(0, H // 256)
+    def _(n):
+        columns = pl.ds(pl.multiple_of(n * 256, 256), 256)
+        hid[:, columns] = jnp.maximum(acc[:, columns], 0.0).astype(BF16)
+
+    @pl.loop(0, G + 3)
+    def _(c):
+        @pl.when(c < G)
+        def _():
+            out_copy(c).wait()
+
+            @pl.loop(0, W // 256)
+            def _(n):
+                columns = pl.ds(pl.multiple_of(n * 256, 256), 256)
+                part[c, :, columns] = dot(hid[...], wout[c, :, columns]).astype(BF16)
+
+            for index in range(4):
+                scatter_hop(index, c).start()
+
+        @pl.when((c >= 1) & (c <= G))
+        def _():
+            k = c - 1
+            scatter_hop(0, k).wait_recv()
+            part[k, 2 * R : 2 * R + h] = (
+                part[k, 2 * R : 2 * R + h].astype(F32) + half[k, 0:h].astype(F32)
+            ).astype(BF16)
+            scatter_hop(5, k).start()
+            scatter_hop(1, k).wait_recv()
+            part[k, R + h : 2 * R] = (
+                part[k, R + h : 2 * R].astype(F32) + half[k, h:R].astype(F32)
+            ).astype(BF16)
+            scatter_hop(4, k).start()
+
+        @pl.when((c >= 2) & (c <= G + 1))
+        def _():
+            k = c - 2
+            for index in range(2, 6):
+                scatter_hop(index, k).wait_recv()
+            summed = (
+                part[k, 0:R].astype(F32) + fin[k, 0:R].astype(F32) + fin[k, R : 2 * R].astype(F32)
+            ).astype(BF16)
+            total = None
+            for q in range(Q):
+                term = dot(pt_mat[q], summed[:, q * S : (q + 1) * S])
+                total = term if total is None else total + term
+            back[k] = total.astype(BF16)
+            exchange_start(back, ret, b_send, b_recv, k)
+
+        @pl.when(c >= 3)
+        def _():
+            k = c - 3
+            exchange_arrived(ret, b_recv, k)
+            for q in range(Q):
+                columns = pl.ds(pl.multiple_of(k * W + q * S, S), S)
+                out[:, columns] = (gate[...] * dot(c_mat[q], ret[k])).astype(BF16)
+
+    @pl.loop(0, G)
+    def _(c):
+        exchange_sent(disp, d_send, c)
+        exchange_sent(back, b_send, c)
+        for index in range(4):
+            gather_hop(index, c).wait_send()
+        for index in range(6):
+            scatter_hop(index, c).wait_send()
+
+
+def fused(tokens, expert_ids, slot_ids, router, w_in, w_out):
+    T, D = tokens.shape
+    E = router.shape[1]
+    C = 5 * T // (4 * E)
+    H = w_in.shape[2]
+    Q = 16 // math.gcd(16, C)
+    G = min(CHUNKS, D // (128 * Q))
+    W = D // G
+    S = W // Q
+    B, R = Q * C, E * C
+    dims = (E, C, Q, G, W, S, T, H)
+    vmem = pl.BlockSpec(memory_space=pltpu.VMEM)
+    hbm = pl.BlockSpec(memory_space=pl.ANY)
+    dma = pltpu.SemaphoreType.DMA
+    return pl.pallas_call(
+        functools.partial(kernel, dims),
+        out_shape=jax.ShapeDtypeStruct((T, D), BF16),
+        in_specs=[vmem, vmem, vmem, vmem, hbm, hbm],
+        out_specs=vmem,
+        scratch_shapes=[
+            pltpu.VMEM((G, E * B, S), BF16),
+            pltpu.VMEM((G, E * B, S), BF16),
+            pltpu.VMEM((G, 4 * R, W), BF16),
+            pltpu.VMEM((4 * R, H), F32),
+            pltpu.VMEM((4 * R, H), BF16),
+            pltpu.VMEM((G, W, H), BF16),
+            pltpu.VMEM((G, H, W), BF16),
+            pltpu.VMEM((G, 4 * R, W), BF16),
+            pltpu.VMEM((G, R, W), BF16),
+            pltpu.VMEM((G, 2 * R, W), BF16),
+            pltpu.VMEM((G, E * B, S), BF16),
+            pltpu.VMEM((G, E * B, S), BF16),
+            pltpu.VMEM((Q, E * B, T), BF16),
+            pltpu.VMEM((Q, R, E * B), BF16),
+            pltpu.VMEM((Q, E * B, R), BF16),
+            pltpu.VMEM((Q, T, E * B), BF16),
+            pltpu.VMEM((T, 1), F32),
+            dma((G,)), dma((G,)), dma((G,)), dma((G,)),
+            dma((4, G)), dma((4, G)), dma((6, G)), dma((6, G)),
+            dma((G,)), dma((G,)),
+        ],
+        compiler_params=pltpu.CompilerParams(
+            collective_id=0, has_side_effects=True, vmem_limit_bytes=62 * 1024 * 1024
+        ),
+        cost_estimate=pl.CostEstimate(
+            flops=16 * R * D * H, bytes_accessed=4 * D * H, transcendentals=T
+        ),
+    )(tokens, expert_ids.reshape(1, T), slot_ids.reshape(1, T), router, w_in, w_out)
+
+
 def solution(mesh):
+    body = fused if mesh.shape["section"] == 4 else per_device
     return jax.shard_map(
-        per_device,
+        body,
         mesh=mesh,
         in_specs=(
             P(("section", "expert"), None),

time: 359 us -> 119 us (0.33)
  waiting for transfers between devices: 161 us -> 0 us
  blocking collectives: 121 us -> 0 us
  Pallas kernels: 0 us -> 114 us
  matrix products: 30.7 us -> 0 us
  local copies, waits for them, and re-layouts: 27.3 us -> 4.44 us
  between operations: 13.4 us -> 0.01 us
  starting transfers between devices: 4.64 us -> 0 us
    all_to_all x1 -> x0, blocking collectives: 121 us -> none  [per_device(): lax.all_to_all(grouped, 'expert', split_axis=1, concat_axis=1, tiled=True)]
    pallas_call x0 -> x1, Pallas kernels: none -> 114 us  [fused(): pl.pallas_call(functools.partial(kernel, dims), out_shape=jax.ShapeDtypeS...]
    all_gather x1 -> x0, waiting for transfers between devices: 64.2 us -> none  [per_device(): grouped = lax.all_gather(dispatch, 'section', axis=0, tiled=True)]
    reduce_scatter x1 -> x0, waiting for transfers between devices: 59.4 us -> none  [per_device(): lax.psum_scatter(jnp.dot(hidden, outward, preferred_element_type=jnp.floa...]
    all_to_all x1 -> x0, waiting for transfers between devices: 37.4 us -> none  [per_device(): lax.all_to_all(expert_out, 'expert', split_axis=0, concat_axis=0, tiled=T...]
    dot_general x4 -> x0, matrix products: 30.7 us -> none  [the longest x1 25.9 us: per_device(): jnp.dot(hidden, outward, preferred_element_type=jnp.float32)]
    reshape x5 -> x0, local copies, waits for them, and re-layouts: 14.7 us -> none  [the longest x1 7.83 us: per_device(): flat = arrived.reshape(-1, width_model)]
    all_gather x1 -> x0, local copies, waits for them, and re-layouts: 6.53 us -> none  [per_device(): grouped = lax.all_gather(dispatch, 'section', axis=0, tiled=True)]
  transfers between devices with their start and end apart: 3 -> 0, of which waited for: 3 -> 0; matrix products, arithmetic and copies ran while one was open for 0% -> 0% of each run, Pallas kernels for 0% -> 0%
where the time goes in v1:
time: 119 us
  Pallas kernels  114 us (96%)
  local copies, waits for them, and re-layouts  4.44 us (4%)
    pallas_call x1, Pallas kernels, fused(): pl.pallas_call(functools.partial(kernel, dims), out_shape=jax.ShapeDtypeS...  114 us
    unnamed x2, local copies, waits for them, and re-layouts  4.44 us

profile of v1, /device:TPU:0, one launch (start us, length us, event | category | flops | bytes accessed | tf_op | source)
XLA Modules:
  0.0 118.5 jit_solution(1870956982337844538)
XLA Ops:
  0.0 2.2 %copy.7.router = bf16[4096,8]{1,0:T(8,128)(2,1)} copy(bf16[4096,8]{0,1:T(8,128)(2,1)} %param.9) | data formatting | bytes 131072 | tf_op args[3]
  2.2 114.1 %shard_map.64 = bf16[128,4096]{1,0:T(8,128)(2,1)} custom-call(bf16[128,4096]{1,0:T(8,128)(2,1)} %tok.1, s32[1,128]{1,0:T(1,128)} %bitcast.2, s32[1,128]{1,0:T(1,128)} %bitcast.3, bf16[4096,8]{1,0:T(8,128)(2,1)} %copy.7.router, bf16[1,4096,1280]{2,1,0:T(8,128)(2,1)} %w_in.1, bf16[1,1280,4096]{2,1,0:T(8,128)(2,1)} %w_out.1), custom_call_target="tpu_custom_call" | custom-call | flops 13421772800 | bytes 20971520 | tf_op jit(solution)/shard_map/pallas_call | solution.py:318
  116.3 2.3 %copy.9 = bf16[128,4096]{1,0:T(8,128)(2,1)} copy(bf16[128,4096]{1,0:T(8,128)(2,1)} %shard_map.64) | data formatting | bytes 2097152

commit v2 on v0

--- a/solution.py
+++ b/solution.py
@@ -1,7 +1,17 @@
+import functools
+import math
+
 import jax
 import jax.numpy as jnp
 from jax import lax
+from jax.experimental import pallas as pl
+from jax.experimental.pallas import tpu as pltpu
 from jax.sharding import PartitionSpec as P
+
+MESH = pl.DeviceIdType.MESH
+BF16 = jnp.bfloat16
+F32 = jnp.float32
+CHUNKS = 8
 
 
 def per_device(tokens, expert_ids, slot_ids, router, w_in, w_out):
@@ -13,12 +23,11 @@
         cell_index[None, :] == jnp.arange(experts * capacity, dtype=jnp.int32)[:, None]
     ).astype(jnp.bfloat16)
     dispatch = jnp.dot(onehot, tokens, preferred_element_type=jnp.float32).astype(jnp.bfloat16)
-    dispatch = dispatch.reshape(1, experts, capacity, width_model)
+    dispatch = dispatch.reshape(experts, capacity, width_model)
     inward = w_in[0]
     outward = w_out[0]
-    grouped = lax.all_gather(dispatch, "section", axis=0, tiled=True)
-    arrived = lax.all_to_all(grouped, "expert", split_axis=1, concat_axis=1, tiled=True)
-    flat = arrived.reshape(-1, width_model)
+    arrived = lax.all_to_all(dispatch, "expert", split_axis=0, concat_axis=0, tiled=True)
+    flat = lax.all_gather(arrived.reshape(-1, width_model), "section", axis=0, tiled=True)
     hidden = jax.nn.relu(jnp.dot(flat, inward, preferred_element_type=jnp.float32)).astype(
         jnp.bfloat16
     )
@@ -42,9 +51,450 @@
     return (gating[:, None] * combined).astype(jnp.bfloat16)
 
 
+def divide(value, number):
+    return lax.shift_right_logical(value * (-(-(1 << 20) // number)), 20)
+
+
+def iota(shape, dim):
+    return lax.broadcasted_iota(jnp.int32, shape, dim)
+
+
+def one_where(condition):
+    return jnp.where(condition, 1.0, 0.0).astype(BF16)
+
+
+def dot(a, b):
+    return jnp.dot(a, b, preferred_element_type=F32)
+
+
+def kernel(
+    dims, tok, eid, sid, router, w_in, w_out, out,
+    near_disp, far_disp, near_x, far_x, x_chunk, acc, hid, win, wout, p_chunk,
+    near_part, far_part, near_half, far_half, near_fin, far_fin,
+    near_back, far_back, near_ret, far_ret,
+    d_mat, p_mat, pt_mat, c_mat, gate, comb, out_v,
+    win_sem, wout_sem, out_sem,
+    near_d_send, near_d_recv, far_d_send, far_d_recv,
+    near_g_send, near_g_recv, far_g_send, far_g_recv,
+    near_s_send, near_s_recv, far_s_send, far_s_recv,
+    near_b_send, near_b_recv, far_b_send, far_b_recv,
+):
+    E, C, Q, G, U, W, S, T, H = dims
+    B, R = Q * C, E * C
+    V = G // U
+    NEAR, FAR = 2 * V * B, (E - 2) * B
+    section, expert = lax.axis_index("section"), lax.axis_index("expert")
+    y, x = section // 2, section % 2
+    core = expert % 2
+    chip = expert - core
+    xn = {"section": y * 2 + (1 - x), "expert": expert}
+    yn = {"section": (1 - y) * 2 + x, "expert": expert}
+    sibling = {"section": section, "expert": chip + 1 - core}
+    far = [({"section": section, "expert": (chip + d) % E}, d) for d in range(2, E)]
+
+    def in_copy(c):
+        return pltpu.make_async_copy(w_in.at[0, pl.ds(c * W, W)], win.at[c], win_sem.at[c])
+
+    def out_copy(c):
+        columns = pl.ds(pl.multiple_of(c * W, W), W)
+        return pltpu.make_async_copy(w_out.at[0, :, columns], wout.at[c], wout_sem.at[c])
+
+    def result_copy(u):
+        columns = pl.ds(pl.multiple_of(u * V * W, V * W), V * W)
+        return pltpu.make_async_copy(out_v.at[:, columns], out.at[:, columns], out_sem.at[u])
+
+    def far_start(src, dst, send, recv, c):
+        for target, d in far:
+            row = pl.multiple_of((core + E - 2 * (d // 2) - 2) * B, 16)
+            pltpu.make_async_remote_copy(
+                src_ref=src.at[c, pl.ds((d - 2) * B, B)],
+                dst_ref=dst.at[c, pl.ds(row, B)],
+                send_sem=send.at[c],
+                recv_sem=recv.at[c],
+                device_id=target,
+                device_id_type=MESH,
+            ).start()
+
+    def near_start(src, dst, send, recv, u):
+        mine = pl.ds(pl.multiple_of(core * (V * B), 16), V * B)
+        other = pl.ds(pl.multiple_of((1 - core) * (V * B), 16), V * B)
+        pltpu.make_async_remote_copy(
+            src_ref=src.at[u, other],
+            dst_ref=dst.at[u, mine],
+            send_sem=send.at[u],
+            recv_sem=recv.at[u],
+            device_id=sibling,
+            device_id_type=MESH,
+        ).start()
+        pltpu.make_async_copy(src.at[u, mine], dst.at[u, mine], recv.at[u]).start()
+
+    def await_rows(ref, sem, index, rows):
+        view = ref.at[index, pl.ds(0, rows)]
+        pltpu.make_async_copy(view, view, sem.at[index]).wait()
+
+    def hop(src, src_row, dst, dst_row, rows, send, recv, index, c, target):
+        return pltpu.make_async_remote_copy(
+            src_ref=src.at[c, pl.ds(src_row, rows)],
+            dst_ref=dst.at[c, pl.ds(dst_row, rows)],
+            send_sem=send.at[index, c],
+            recv_sem=recv.at[index, c],
+            device_id=target,
+            device_id_type=MESH,
+        )
+
+    def gather_hop(buffers, index, c):
+        held, n, send, recv = buffers
+        h = n // 2
+        src_row, dst_row, rows, target = (
+            (0, n, n, xn),
+            (0, 2 * n, n, yn),
+            (n, 3 * n, h, yn),
+            (2 * n + h, 3 * n + h, h, xn),
+        )[index]
+        return hop(held, src_row, held, dst_row, rows, send, recv, index, c, target)
+
+    def scatter_hop(buffers, index, c):
+        part, half, fin, n, send, recv = buffers
+        h = n // 2
+        src_row, dst, dst_row, target = (
+            (3 * n, half, 0, xn),
+            (3 * n + h, half, h, yn),
+            (n, fin, 0, xn),
+            (2 * n + h, fin, n + h, yn),
+            (n + h, fin, h, xn),
+            (2 * n, fin, n, yn),
+        )[index]
+        return hop(part, src_row, dst, dst_row, h, send, recv, index, c, target)
+
+    near_g = (near_x, NEAR, near_g_send, near_g_recv)
+    far_g = (far_x, FAR, far_g_send, far_g_recv)
+    near_s = (near_part, near_half, near_fin, NEAR, near_s_send, near_s_recv)
+    far_s = (far_part, far_half, far_fin, FAR, far_s_send, far_s_recv)
+
+    def gather_own(buffers, c):
+        gather_hop(buffers, 0, c).start()
+        gather_hop(buffers, 1, c).start()
+
+    def gather_relay(buffers, c):
+        gather_hop(buffers, 0, c).wait_recv()
+        gather_hop(buffers, 2, c).start()
+        gather_hop(buffers, 1, c).wait_recv()
+        gather_hop(buffers, 3, c).start()
+
+    def gather_rest(buffers, c):
+        gather_hop(buffers, 2, c).wait_recv()
+        gather_hop(buffers, 3, c).wait_recv()
+
+    def scatter_own(buffers, c):
+        for index in range(4):
+            scatter_hop(buffers, index, c).start()
+
+    def scatter_relay(buffers, c):
+        part, half, _, n, _, _ = buffers
+        h = n // 2
+        for wait, row, at, send in ((0, 2 * n, 0, 5), (1, n + h, h, 4)):
+            scatter_hop(buffers, wait, c).wait_recv()
+            part[c, row : row + h] = (
+                part[c, row : row + h].astype(F32) + half[c, at : at + h].astype(F32)
+            ).astype(BF16)
+            scatter_hop(buffers, send, c).start()
+
+    def scatter_total(buffers, c, back):
+        part, _, fin, n, _, _ = buffers
+        for index in range(2, 6):
+            scatter_hop(buffers, index, c).wait_recv()
+        back[c] = (
+            part[c, 0:n].astype(F32) + fin[c, 0:n].astype(F32) + fin[c, n : 2 * n].astype(F32)
+        ).astype(BF16)
+
+    barrier = pltpu.get_barrier_semaphore()
+    for target in [target for target, _ in far] + [sibling, xn, yn]:
+        pl.semaphore_signal(barrier, inc=1, device_id=target, device_id_type=MESH)
+
+    def keys(shape, dim, first):
+        r = iota(shape, dim)
+        block = divide(r, B)
+        inner = r - block * B
+        quarter = divide(inner, C)
+        owner = block + first
+        owner = jnp.where(owner >= E, owner - E, owner)
+        return quarter * R + owner * C + (inner - quarter * C)
+
+    cell_row = eid[...] * C + sid[...]
+    diagonal = iota((T, T), 0) == iota((T, T), 1)
+
+    def column(row):
+        spread = jnp.where(diagonal, jnp.broadcast_to(row, (T, T)), 0).astype(F32)
+        return jnp.sum(spread, axis=1, keepdims=True).astype(jnp.int32)
+
+    key = keys((E * B, T), 0, chip)
+    for q in range(Q):
+        d_mat[:, q * T : (q + 1) * T] = one_where(key == cell_row + q * R)
+
+    def stacked(c):
+        return jnp.concatenate(
+            [tok[:, pl.ds(pl.multiple_of(c * W + q * S, S), S)] for q in range(Q)], axis=0
+        )
+
+    def far_dispatch(c):
+        far_disp[c] = dot(d_mat[2 * B :], stacked(c)).astype(BF16)
+        far_start(far_disp, far_x, far_d_send, far_d_recv, c)
+
+    for u in range(U):
+        for v in range(V):
+            rows = dot(d_mat[0 : 2 * B], stacked(u * V + v)).astype(BF16)
+            near_disp[u, v * B : (v + 1) * B] = rows[0:B]
+            near_disp[u, (V + v) * B : (V + v + 1) * B] = rows[B : 2 * B]
+    pl.semaphore_wait(barrier, E + 1)
+    for u in range(U):
+        near_start(near_disp, near_x, near_d_send, near_d_recv, u)
+    far_dispatch(0)
+    for u in range(U):
+        await_rows(near_x, near_d_recv, u, NEAR)
+        gather_own(near_g, u)
+    far_dispatch(1)
+
+    @pl.loop(0, G)
+    def _(c):
+        in_copy(c).start()
+
+    key = keys((R * Q, E * B), 1, 0)
+    p_mat[...] = one_where(key == iota((R * Q, E * B), 0))
+    acc[...] = jnp.zeros_like(acc)
+
+    def near_rows(ref, k, base):
+        u, v = k // V, k % V
+        first = pl.multiple_of(base + v * B, 16)
+        second = pl.multiple_of(base + (V + v) * B, 16)
+        return [ref[u, pl.ds(first, B)], ref[u, pl.ds(second, B)]]
+
+    @pl.loop(0, G + 3)
+    def _(c):
+        @pl.when(c + 2 < G)
+        def _():
+            far_dispatch(c + 2)
+
+        @pl.when(c < G)
+        def _():
+            out_copy(c).start()
+            await_rows(far_x, far_d_recv, c, FAR)
+            gather_own(far_g, c)
+
+        @pl.when(c < U)
+        def _():
+            gather_relay(near_g, c)
+
+        @pl.when(c == 0)
+        def _():
+            key = keys((E * B, R * Q), 0, 0)
+            pt_mat[...] = one_where(key == iota((E * B, R * Q), 1))
+            key = keys((T, E * B), 1, chip)
+            cell_column = column(cell_row)
+            for q in range(Q):
+                c_mat[q * T : (q + 1) * T] = one_where(key == cell_column + q * R)
+            logits = lax.dot_general(
+                tok[...], router[...], (((1,), (1,)), ((), ())), preferred_element_type=F32
+            )
+            chosen = column(eid[...]) == iota((T, E), 1)
+            picked = jnp.sum(jnp.where(chosen, logits, 0.0), axis=1, keepdims=True)
+            gate[...] = 1.0 / (1.0 + jnp.exp(-picked))
+
+        @pl.when((c >= 2) & (c < G + 2))
+        def _():
+            gather_relay(far_g, c - 2)
+
+        @pl.when(c == 2)
+        def _():
+            for u in range(U):
+                gather_rest(near_g, u)
+
+        @pl.when(c >= 3)
+        def _():
+            k = c - 3
+            gather_rest(far_g, k)
+            raw = [
+                jnp.concatenate(
+                    near_rows(near_x, k, s * NEAR) + [far_x[k, s * FAR : (s + 1) * FAR]], axis=0
+                )
+                for s in range(4)
+            ]
+            moved = dot(p_mat[...], jnp.concatenate(raw, axis=1)).astype(BF16)
+            for s in range(4):
+                for q in range(Q):
+                    x_chunk[s * R : (s + 1) * R, q * S : (q + 1) * S] = moved[
+                        q * R : (q + 1) * R, s * S : (s + 1) * S
+                    ]
+            in_copy(k).wait()
+
+            @pl.loop(0, H // 256)
+            def _(n):
+                columns = pl.ds(pl.multiple_of(n * 256, 256), 256)
+                acc[:, columns] += dot(x_chunk[...], win[k, :, columns])
+
+    @pl.loop(0, H // 256)
+    def _(n):
+        columns = pl.ds(pl.multiple_of(n * 256, 256), 256)
+        hid[:, columns] = jnp.maximum(acc[:, columns], 0.0).astype(BF16)
+
+    def combine_near(u):
+        await_rows(near_ret, near_b_recv, u, NEAR)
+        for v in range(V):
+            rows = jnp.concatenate(near_rows(near_ret, u * V + v, 0), axis=0)
+            term = dot(c_mat[:, 0 : 2 * B], rows)
+            for q in range(Q):
+                at = (u * V + v) * W + q * S
+                out_v[:, at : at + S] = (
+                    gate[...] * (comb[:, at : at + S] + term[q * T : (q + 1) * T])
+                ).astype(BF16)
+        result_copy(u).start()
+
+    def when_unit(index, near_step, far_step):
+        @pl.when((index >= 0) & (index < G))
+        def _():
+            far_step(index)
+
+        @pl.when((index >= G) & (index < G + U))
+        def _():
+            near_step(index - G)
+
+    def far_own(c):
+        out_copy(c).wait()
+
+        @pl.loop(0, W // 256)
+        def _(n):
+            columns = pl.ds(pl.multiple_of(n * 256, 256), 256)
+            p_chunk[:, columns] = dot(hid[...], wout[c, :, columns]).astype(BF16)
+
+        rows = [
+            jnp.concatenate(
+                [p_chunk[s * R : (s + 1) * R, q * S : (q + 1) * S] for s in range(4)], axis=1
+            )
+            for q in range(Q)
+        ]
+        moved = dot(pt_mat[...], jnp.concatenate(rows, axis=0)).astype(BF16)
+        u, v = c // V, c % V
+        for s in range(4):
+            columns = slice(s * S, (s + 1) * S)
+            far_part[c, s * FAR : (s + 1) * FAR] = moved[2 * B :, columns]
+            first = pl.multiple_of(s * NEAR + v * B, 16)
+            second = pl.multiple_of(s * NEAR + (V + v) * B, 16)
+            near_part[u, pl.ds(first, B)] = moved[0:B, columns]
+            near_part[u, pl.ds(second, B)] = moved[B : 2 * B, columns]
+        scatter_own(far_s, c)
+
+    def far_total(c):
+        scatter_total(far_s, c, far_back)
+        far_start(far_back, far_ret, far_b_send, far_b_recv, c)
+
+    def near_total(u):
+        scatter_total(near_s, u, near_back)
+        near_start(near_back, near_ret, near_b_send, near_b_recv, u)
+
+    def far_combine(c):
+        await_rows(far_ret, far_b_recv, c, FAR)
+        term = dot(c_mat[:, 2 * B :], far_ret[c])
+        for q in range(Q):
+            columns = pl.ds(pl.multiple_of(c * W + q * S, S), S)
+            comb[:, columns] = term[q * T : (q + 1) * T]
+
+    @pl.loop(0, G + U + 3)
+    def _(c):
+        when_unit(c, lambda u: scatter_own(near_s, u), far_own)
+        when_unit(
+            c - 2, lambda u: scatter_relay(near_s, u), lambda k: scatter_relay(far_s, k)
+        )
+        when_unit(c - 3, near_total, far_total)
+
+        @pl.when(c >= U + 3)
+        def _():
+            far_combine(c - U - 3)
+
+    for u in range(U):
+        combine_near(u)
+
+    @pl.loop(0, G)
+    def _(c):
+        await_rows(far_disp, far_d_send, c, FAR)
+        await_rows(far_back, far_b_send, c, FAR)
+        for index in range(4):
+            gather_hop(far_g, index, c).wait_send()
+        for index in range(6):
+            scatter_hop(far_s, index, c).wait_send()
+
+    for u in range(U):
+        await_rows(near_disp, near_d_send, u, V * B)
+        await_rows(near_back, near_b_send, u, V * B)
+        for index in range(4):
+            gather_hop(near_g, index, u).wait_send()
+        for index in range(6):
+            scatter_hop(near_s, index, u).wait_send()
+        result_copy(u).wait()
+
+
+def fused(tokens, expert_ids, slot_ids, router, w_in, w_out):
+    T, D = tokens.shape
+    E = router.shape[1]
+    C = 5 * T // (4 * E)
+    H = w_in.shape[2]
+    Q = 16 // math.gcd(16, C)
+    G = min(CHUNKS, D // (128 * Q))
+    U = 2
+    W = D // G
+    S = W // Q
+    B, R = Q * C, E * C
+    NEAR, FAR = 2 * (G // U) * B, (E - 2) * B
+    dims = (E, C, Q, G, U, W, S, T, H)
+    vmem = pl.BlockSpec(memory_space=pltpu.VMEM)
+    hbm = pl.BlockSpec(memory_space=pl.ANY)
+    dma = pltpu.SemaphoreType.DMA
+    rows = lambda near, far: [pltpu.VMEM((U, near, S), BF16), pltpu.VMEM((G, far, S), BF16)]
+    return pl.pallas_call(
+        functools.partial(kernel, dims),
+        out_shape=jax.ShapeDtypeStruct((T, D), BF16),
+        in_specs=[vmem, vmem, vmem, vmem, hbm, hbm],
+        out_specs=hbm,
+        scratch_shapes=rows(NEAR, FAR)
+        + rows(4 * NEAR, 4 * FAR)
+        + [
+            pltpu.VMEM((4 * R, W), BF16),
+            pltpu.VMEM((4 * R, H), F32),
+            pltpu.VMEM((4 * R, H), BF16),
+            pltpu.VMEM((G, W, H), BF16),
+            pltpu.VMEM((G, H, W), BF16),
+            pltpu.VMEM((4 * R, W), BF16),
+        ]
+        + rows(4 * NEAR, 4 * FAR)
+        + rows(NEAR, FAR)
+        + rows(2 * NEAR, 2 * FAR)
+        + rows(NEAR, FAR)
+        + rows(NEAR, FAR)
+        + [
+            pltpu.VMEM((E * B, Q * T), BF16),
+            pltpu.VMEM((Q * R, E * B), BF16),
+            pltpu.VMEM((E * B, Q * R), BF16),
+            pltpu.VMEM((Q * T, E * B), BF16),
+            pltpu.VMEM((T, 1), F32),
+            pltpu.VMEM((T, D), F32),
+            pltpu.VMEM((T, D), BF16),
+        ]
+        + [dma((G,)), dma((G,)), dma((U,))]
+        + [dma((n,)) for n in (U, U, G, G)]
+        + [dma((4, n)) for n in (U, U, G, G)]
+        + [dma((6, n)) for n in (U, U, G, G)]
+        + [dma((n,)) for n in (U, U, G, G)],
+        compiler_params=pltpu.CompilerParams(
+            collective_id=0, has_side_effects=True, vmem_limit_bytes=62 * 1024 * 1024
+        ),
+        cost_estimate=pl.CostEstimate(
+            flops=16 * R * D * H, bytes_accessed=4 * D * H, transcendentals=T
+        ),
+    )(tokens, expert_ids.reshape(1, T), slot_ids.reshape(1, T), router.T, w_in, w_out)
+
+
 def solution(mesh):
+    body = fused if mesh.shape["section"] == 4 else per_device
     return jax.shard_map(
-        per_device,
+        body,
         mesh=mesh,
         in_specs=(
             P(("section", "expert"), None),

time: 359 us -> 114 us (0.32)
  waiting for transfers between devices: 161 us -> 0 us
  blocking collectives: 121 us -> 0 us
  Pallas kernels: 0 us -> 111 us
  matrix products: 30.7 us -> 0 us
  local copies, waits for them, and re-layouts: 27.3 us -> 2.29 us
  between operations: 13.4 us -> 0.01 us
  starting transfers between devices: 4.64 us -> 0 us
    all_to_all x1 -> x0, blocking collectives: 121 us -> none  [per_device(): lax.all_to_all(grouped, 'expert', split_axis=1, concat_axis=1, tiled=True)]
    pallas_call x0 -> x1, Pallas kernels: none -> 111 us  [fused(): pl.pallas_call(functools.partial(kernel, dims), out_shape=jax.ShapeDtypeS...]
    all_gather x1 -> x0, waiting for transfers between devices: 64.2 us -> none  [per_device(): grouped = lax.all_gather(dispatch, 'section', axis=0, tiled=True)]
    reduce_scatter x1 -> x0, waiting for transfers between devices: 59.4 us -> none  [per_device(): lax.psum_scatter(jnp.dot(hidden, outward, preferred_element_type=jnp.floa...]
    all_to_all x1 -> x0, waiting for transfers between devices: 37.4 us -> none  [per_device(): lax.all_to_all(expert_out, 'expert', split_axis=0, concat_axis=0, tiled=T...]
    dot_general x4 -> x0, matrix products: 30.7 us -> none  [the longest x1 25.9 us: per_device(): jnp.dot(hidden, outward, preferred_element_type=jnp.float32)]
    reshape x5 -> x0, local copies, waits for them, and re-layouts: 14.7 us -> none  [the longest x1 7.83 us: per_device(): flat = arrived.reshape(-1, width_model)]
    all_gather x1 -> x0, local copies, waits for them, and re-layouts: 6.53 us -> none  [per_device(): grouped = lax.all_gather(dispatch, 'section', axis=0, tiled=True)]
  transfers between devices with their start and end apart: 3 -> 0, of which waited for: 3 -> 0; matrix products, arithmetic and copies ran while one was open for 0% -> 0% of each run, Pallas kernels for 0% -> 0%
where the time goes in v2:
time: 114 us; the launch traced here: 113 us
  Pallas kernels  111 us (97%)
  local copies, waits for them, and re-layouts  2.29 us (2%)
    pallas_call x1, Pallas kernels, fused(): pl.pallas_call(functools.partial(kernel, dims), out_shape=jax.ShapeDtypeS...  111 us
    unnamed x1, local copies, waits for them, and re-layouts  2.29 us

profile of v2, /device:TPU:0, one launch (start us, length us, event | category | flops | bytes accessed | tf_op | source)
XLA Modules:
  0.0 113.4 jit_solution(13402744201402724526)
XLA Ops:
  0.0 111.1 %shard_map.64 = bf16[128,4096]{1,0:T(8,128)(2,1)} custom-call(bf16[128,4096]{1,0:T(8,128)(2,1)} %tok.1, s32[1,128]{1,0:T(1,128)} %bitcast.4, s32[1,128]{1,0:T(1,128)} %bitcast.5, bf16[8,4096]{1,0:T(8,128)(2,1)} %bitcast.3, bf16[1,4096,1280]{2,1,0:T(8,128)(2,1)} %w_in.1, bf16[1,1280,4096]{2,1,0:T(8,128)(2,1)} %w_out.1), custom_call_target="tpu_custom_call" | custom-call | flops 13421772800 | bytes 20971520 | tf_op jit(solution)/shard_map/pallas_call | solution.py:451
  111.1 2.3 %copy.8 = bf16[128,4096]{1,0:T(8,128)(2,1)} copy(bf16[128,4096]{1,0:T(8,128)(2,1)} %shard_map.64) | data formatting | bytes 2097152

commit v3 on v2

--- a/solution.py
+++ b/solution.py
@@ -69,17 +69,17 @@
 
 def kernel(
     dims, tok, eid, sid, router, w_in, w_out, out,
-    near_disp, far_disp, near_x, far_x, x_chunk, acc, hid, win, wout, p_chunk,
+    near_disp, far_disp, near_x, far_x, near_chunk, far_chunk, near_acc, far_acc, near_hid, far_hid, win, wout,
     near_part, far_part, near_half, far_half, near_fin, far_fin,
     near_back, far_back, near_ret, far_ret,
-    d_mat, p_mat, pt_mat, c_mat, gate, comb, out_v,
-    win_sem, wout_sem, out_sem,
+    d_mat, near_p, far_p, near_pt, far_pt, c_mat, gate, comb,
+    win_sem, wout_sem,
     near_d_send, near_d_recv, far_d_send, far_d_recv,
     near_g_send, near_g_recv, far_g_send, far_g_recv,
     near_s_send, near_s_recv, far_s_send, far_s_recv,
     near_b_send, near_b_recv, far_b_send, far_b_recv,
 ):
-    E, C, Q, G, U, W, S, T, H = dims
+    E, C, Q, G, U, W, S, T, H, NP, FP = dims
     B, R = Q * C, E * C
     V = G // U
     NEAR, FAR = 2 * V * B, (E - 2) * B
@@ -98,10 +98,6 @@
     def out_copy(c):
         columns = pl.ds(pl.multiple_of(c * W, W), W)
         return pltpu.make_async_copy(w_out.at[0, :, columns], wout.at[c], wout_sem.at[c])
-
-    def result_copy(u):
-        columns = pl.ds(pl.multiple_of(u * V * W, V * W), V * W)
-        return pltpu.make_async_copy(out_v.at[:, columns], out.at[:, columns], out_sem.at[u])
 
     def far_start(src, dst, send, recv, c):
         for target, d in far:
@@ -211,14 +207,14 @@
     for target in [target for target, _ in far] + [sibling, xn, yn]:
         pl.semaphore_signal(barrier, inc=1, device_id=target, device_id_type=MESH)
 
-    def keys(shape, dim, first):
+    def keys(shape, dim, first, stride):
         r = iota(shape, dim)
         block = divide(r, B)
         inner = r - block * B
         quarter = divide(inner, C)
         owner = block + first
         owner = jnp.where(owner >= E, owner - E, owner)
-        return quarter * R + owner * C + (inner - quarter * C)
+        return quarter * stride + owner * C + (inner - quarter * C)
 
     cell_row = eid[...] * C + sid[...]
     diagonal = iota((T, T), 0) == iota((T, T), 1)
@@ -227,7 +223,7 @@
         spread = jnp.where(diagonal, jnp.broadcast_to(row, (T, T)), 0).astype(F32)
         return jnp.sum(spread, axis=1, keepdims=True).astype(jnp.int32)
 
-    key = keys((E * B, T), 0, chip)
+    key = keys((E * B, T), 0, chip, R)
     for q in range(Q):
         d_mat[:, q * T : (q + 1) * T] = one_where(key == cell_row + q * R)
 
@@ -240,27 +236,89 @@
         far_disp[c] = dot(d_mat[2 * B :], stacked(c)).astype(BF16)
         far_start(far_disp, far_x, far_d_send, far_d_recv, c)
 
-    for u in range(U):
+    def near_dispatch(u):
         for v in range(V):
             rows = dot(d_mat[0 : 2 * B], stacked(u * V + v)).astype(BF16)
             near_disp[u, v * B : (v + 1) * B] = rows[0:B]
             near_disp[u, (V + v) * B : (V + v + 1) * B] = rows[B : 2 * B]
+
+    near_dispatch(0)
     pl.semaphore_wait(barrier, E + 1)
-    for u in range(U):
+    near_start(near_disp, near_x, near_d_send, near_d_recv, 0)
+    for u in range(1, U):
+        near_dispatch(u)
         near_start(near_disp, near_x, near_d_send, near_d_recv, u)
-    far_dispatch(0)
     for u in range(U):
         await_rows(near_x, near_d_recv, u, NEAR)
         gather_own(near_g, u)
-    far_dispatch(1)
+        far_dispatch(u)
 
     @pl.loop(0, G)
     def _(c):
         in_copy(c).start()
 
-    key = keys((R * Q, E * B), 1, 0)
-    p_mat[...] = one_where(key == iota((R * Q, E * B), 0))
-    acc[...] = jnp.zeros_like(acc)
+    def order(p, pt, rows, stride):
+        p[...] = one_where(keys((Q * stride, rows), 1, 0, stride) == iota((Q * stride, rows), 0))
+        pt[...] = one_where(keys((rows, Q * stride), 0, 0, stride) == iota((rows, Q * stride), 1))
+
+    order(near_p, near_pt, 2 * B, NP)
+    order(far_p, far_pt, FAR, FP)
+    near_acc[...] = jnp.zeros_like(near_acc)
+    far_acc[...] = jnp.zeros_like(far_acc)
+
+    def widen(raw, p, chunk, stride):
+        moved = dot(p[...], jnp.concatenate(raw, axis=1)).astype(BF16)
+        for s in range(4):
+            for q in range(Q):
+                chunk[s * stride : (s + 1) * stride, q * S : (q + 1) * S] = moved[
+                    q * stride : (q + 1) * stride, s * S : (s + 1) * S
+                ]
+
+    def narrow(chunk, pt, stride):
+        rows = [
+            jnp.concatenate(
+                [chunk[s * stride : (s + 1) * stride, q * S : (q + 1) * S] for s in range(4)],
+                axis=1,
+            )
+            for q in range(Q)
+        ]
+        return dot(pt[...], jnp.concatenate(rows, axis=0)).astype(BF16)
+
+    def inward(acc, chunk, k):
+        @pl.loop(0, H // 256)
+        def _(n):
+            columns = pl.ds(pl.multiple_of(n * 256, 256), 256)
+            acc[:, columns] += dot(chunk[...], win[k, :, columns])
+
+    def activate(acc, hid):
+        @pl.loop(0, H // 256)
+        def _(n):
+            columns = pl.ds(pl.multiple_of(n * 256, 256), 256)
+            hid[:, columns] = jnp.maximum(acc[:, columns], 0.0).astype(BF16)
+
+    def outward(hid, chunk, k):
+        @pl.loop(0, W // 256)
+        def _(n):
+            columns = pl.ds(pl.multiple_of(n * 256, 256), 256)
+            chunk[:, columns] = dot(hid[...], wout[k, :, columns]).astype(BF16)
+
+    def near_inward(k):
+        raw = [jnp.concatenate(near_rows(near_x, k, s * NEAR), axis=0) for s in range(4)]
+        widen(raw, near_p, near_chunk, NP)
+        in_copy(k).wait()
+        inward(near_acc, near_chunk, k)
+
+    def near_outward(k):
+        out_copy(k).wait()
+        outward(near_hid, near_chunk, k)
+        moved = narrow(near_chunk, near_pt, NP)
+        u, v = k // V, k % V
+        for s in range(4):
+            columns = slice(s * S, (s + 1) * S)
+            first = pl.multiple_of(s * NEAR + v * B, 16)
+            second = pl.multiple_of(s * NEAR + (V + v) * B, 16)
+            near_part[u, pl.ds(first, B)] = moved[0:B, columns]
+            near_part[u, pl.ds(second, B)] = moved[B : 2 * B, columns]
 
     def near_rows(ref, k, base):
         u, v = k // V, k % V
@@ -286,9 +344,7 @@
 
         @pl.when(c == 0)
         def _():
-            key = keys((E * B, R * Q), 0, 0)
-            pt_mat[...] = one_where(key == iota((E * B, R * Q), 1))
-            key = keys((T, E * B), 1, chip)
+            key = keys((T, E * B), 1, chip, R)
             cell_column = column(cell_row)
             for q in range(Q):
                 c_mat[q * T : (q + 1) * T] = one_where(key == cell_column + q * R)
@@ -308,33 +364,32 @@
             for u in range(U):
                 gather_rest(near_g, u)
 
+        @pl.when(c == G + 1)
+        def _():
+            scatter_own(near_s, 0)
+
+        @pl.when((c >= 3) & (c < 3 + G // 2))
+        def _():
+            for i in range(2):
+                near_inward(2 * (c - 3) + i)
+
+        @pl.when(c == 3 + G // 2)
+        def _():
+            activate(near_acc, near_hid)
+
+        @pl.when((c >= 3 + G // 2) & (c < 3 + G // 2 + V // 2))
+        def _():
+            for i in range(2):
+                near_outward(2 * (c - 3 - G // 2) + i)
+
         @pl.when(c >= 3)
         def _():
             k = c - 3
             gather_rest(far_g, k)
-            raw = [
-                jnp.concatenate(
-                    near_rows(near_x, k, s * NEAR) + [far_x[k, s * FAR : (s + 1) * FAR]], axis=0
-                )
-                for s in range(4)
-            ]
-            moved = dot(p_mat[...], jnp.concatenate(raw, axis=1)).astype(BF16)
-            for s in range(4):
-                for q in range(Q):
-                    x_chunk[s * R : (s + 1) * R, q * S : (q + 1) * S] = moved[
-                        q * R : (q + 1) * R, s * S : (s + 1) * S
-                    ]
-            in_copy(k).wait()
-
-            @pl.loop(0, H // 256)
-            def _(n):
-                columns = pl.ds(pl.multiple_of(n * 256, 256), 256)
-                acc[:, columns] += dot(x_chunk[...], win[k, :, columns])
-
-    @pl.loop(0, H // 256)
-    def _(n):
-        columns = pl.ds(pl.multiple_of(n * 256, 256), 256)
-        hid[:, columns] = jnp.maximum(acc[:, columns], 0.0).astype(BF16)
+            widen([far_x[k, s * FAR : (s + 1) * FAR] for s in range(4)], far_p, far_chunk, FP)
+            inward(far_acc, far_chunk, k)
+
+    activate(far_acc, far_hid)
 
     def combine_near(u):
         await_rows(near_ret, near_b_recv, u, NEAR)
@@ -343,43 +398,15 @@
             term = dot(c_mat[:, 0 : 2 * B], rows)
             for q in range(Q):
                 at = (u * V + v) * W + q * S
-                out_v[:, at : at + S] = (
+                out[:, at : at + S] = (
                     gate[...] * (comb[:, at : at + S] + term[q * T : (q + 1) * T])
                 ).astype(BF16)
-        result_copy(u).start()
-
-    def when_unit(index, near_step, far_step):
-        @pl.when((index >= 0) & (index < G))
-        def _():
-            far_step(index)
-
-        @pl.when((index >= G) & (index < G + U))
-        def _():
-            near_step(index - G)
 
     def far_own(c):
-        out_copy(c).wait()
-
-        @pl.loop(0, W // 256)
-        def _(n):
-            columns = pl.ds(pl.multiple_of(n * 256, 256), 256)
-            p_chunk[:, columns] = dot(hid[...], wout[c, :, columns]).astype(BF16)
-
-        rows = [
-            jnp.concatenate(
-                [p_chunk[s * R : (s + 1) * R, q * S : (q + 1) * S] for s in range(4)], axis=1
-            )
-            for q in range(Q)
-        ]
-        moved = dot(pt_mat[...], jnp.concatenate(rows, axis=0)).astype(BF16)
-        u, v = c // V, c % V
+        outward(far_hid, far_chunk, c)
+        moved = narrow(far_chunk, far_pt, FP)
         for s in range(4):
-            columns = slice(s * S, (s + 1) * S)
-            far_part[c, s * FAR : (s + 1) * FAR] = moved[2 * B :, columns]
-            first = pl.multiple_of(s * NEAR + v * B, 16)
-            second = pl.multiple_of(s * NEAR + (V + v) * B, 16)
-            near_part[u, pl.ds(first, B)] = moved[0:B, columns]
-            near_part[u, pl.ds(second, B)] = moved[B : 2 * B, columns]
+            far_part[c, s * FAR : (s + 1) * FAR] = moved[:, s * S : (s + 1) * S]
         scatter_own(far_s, c)
 
     def far_total(c):
@@ -397,20 +424,53 @@
             columns = pl.ds(pl.multiple_of(c * W + q * S, S), S)
             comb[:, columns] = term[q * T : (q + 1) * T]
 
-    @pl.loop(0, G + U + 3)
+    @pl.loop(0, G + 4)
     def _(c):
-        when_unit(c, lambda u: scatter_own(near_s, u), far_own)
-        when_unit(
-            c - 2, lambda u: scatter_relay(near_s, u), lambda k: scatter_relay(far_s, k)
-        )
-        when_unit(c - 3, near_total, far_total)
-
-        @pl.when(c >= U + 3)
-        def _():
-            far_combine(c - U - 3)
-
-    for u in range(U):
-        combine_near(u)
+        @pl.when(c < G)
+        def _():
+            far_own(c)
+
+        @pl.when(c == G)
+        def _():
+            scatter_own(near_s, 1)
+
+        @pl.when(c == 0)
+        def _():
+            scatter_relay(near_s, 0)
+
+        @pl.when((c >= 2) & (c < G + 2))
+        def _():
+            scatter_relay(far_s, c - 2)
+
+        @pl.when(c == G + 2)
+        def _():
+            scatter_relay(near_s, 1)
+
+        @pl.when(c < G - V)
+        def _():
+            near_outward(V + c)
+
+        @pl.when(c == 2)
+        def _():
+            near_total(0)
+
+        @pl.when((c >= 3) & (c < G + 3))
+        def _():
+            far_total(c - 3)
+
+        @pl.when(c == G + 3)
+        def _():
+            near_total(1)
+
+        @pl.when(c >= 4)
+        def _():
+            far_combine(c - 4)
+
+        @pl.when(c == G)
+        def _():
+            combine_near(0)
+
+    combine_near(1)
 
     @pl.loop(0, G)
     def _(c):
@@ -428,7 +488,6 @@
             gather_hop(near_g, index, u).wait_send()
         for index in range(6):
             scatter_hop(near_s, index, u).wait_send()
-        result_copy(u).wait()
 
 
 def fused(tokens, expert_ids, slot_ids, router, w_in, w_out):
@@ -443,25 +502,28 @@
     S = W // Q
     B, R = Q * C, E * C
     NEAR, FAR = 2 * (G // U) * B, (E - 2) * B
-    dims = (E, C, Q, G, U, W, S, T, H)
+    NP, FP = -(-2 * C // 16) * 16, -(-(E - 2) * C // 16) * 16
+    dims = (E, C, Q, G, U, W, S, T, H, NP, FP)
     vmem = pl.BlockSpec(memory_space=pltpu.VMEM)
     hbm = pl.BlockSpec(memory_space=pl.ANY)
     dma = pltpu.SemaphoreType.DMA
     rows = lambda near, far: [pltpu.VMEM((U, near, S), BF16), pltpu.VMEM((G, far, S), BF16)]
     return pl.pallas_call(
         functools.partial(kernel, dims),
-        out_shape=jax.ShapeDtypeStruct((T, D), BF16),
+        out_shape=pltpu.VMEM((T, D), BF16),
         in_specs=[vmem, vmem, vmem, vmem, hbm, hbm],
-        out_specs=hbm,
+        out_specs=vmem,
         scratch_shapes=rows(NEAR, FAR)
         + rows(4 * NEAR, 4 * FAR)
         + [
-            pltpu.VMEM((4 * R, W), BF16),
-            pltpu.VMEM((4 * R, H), F32),
-            pltpu.VMEM((4 * R, H), BF16),
+            pltpu.VMEM((4 * NP, W), BF16),
+            pltpu.VMEM((4 * FP, W), BF16),
+            pltpu.VMEM((4 * NP, H), F32),
+            pltpu.VMEM((4 * FP, H), F32),
+            pltpu.VMEM((4 * NP, H), BF16),
+            pltpu.VMEM((4 * FP, H), BF16),
             pltpu.VMEM((G, W, H), BF16),
             pltpu.VMEM((G, H, W), BF16),
-            pltpu.VMEM((4 * R, W), BF16),
         ]
         + rows(4 * NEAR, 4 * FAR)
         + rows(NEAR, FAR)
@@ -470,20 +532,21 @@
         + rows(NEAR, FAR)
         + [
             pltpu.VMEM((E * B, Q * T), BF16),
-            pltpu.VMEM((Q * R, E * B), BF16),
-            pltpu.VMEM((E * B, Q * R), BF16),
+            pltpu.VMEM((Q * NP, 2 * B), BF16),
+            pltpu.VMEM((Q * FP, FAR), BF16),
+            pltpu.VMEM((2 * B, Q * NP), BF16),
+            pltpu.VMEM((FAR, Q * FP), BF16),
             pltpu.VMEM((Q * T, E * B), BF16),
             pltpu.VMEM((T, 1), F32),
             pltpu.VMEM((T, D), F32),
-            pltpu.VMEM((T, D), BF16),
         ]
-        + [dma((G,)), dma((G,)), dma((U,))]
+        + [dma((G,)), dma((G,))]
         + [dma((n,)) for n in (U, U, G, G)]
         + [dma((4, n)) for n in (U, U, G, G)]
         + [dma((6, n)) for n in (U, U, G, G)]
         + [dma((n,)) for n in (U, U, G, G)],
         compiler_params=pltpu.CompilerParams(
-            collective_id=0, has_side_effects=True, vmem_limit_bytes=62 * 1024 * 1024
+            collective_id=0, has_side_effects=True, vmem_limit_bytes=56 * 1024 * 1024
         ),
         cost_estimate=pl.CostEstimate(
             flops=16 * R * D * H, bytes_accessed=4 * D * H, transcendentals=T

time: 114 us -> 113 us (level)
  local copies, waits for them, and re-layouts: 2.29 us -> 0.97 us
    unnamed x1, local copies, waits for them, and re-layouts: 2.29 us -> 0.97 us
    pallas_call x1, Pallas kernels: 111 us -> 112 us  [fused(): pl.pallas_call(functools.partial(kernel, dims), out_shape=pltpu.VMEM((T,...]
where the time goes in v3:
time: 113 us
  Pallas kernels  112 us (99%)
    pallas_call x1, Pallas kernels, fused(): pl.pallas_call(functools.partial(kernel, dims), out_shape=pltpu.VMEM((T,...  112 us

profile of v3, /device:TPU:0, one launch (start us, length us, event | category | flops | bytes accessed | tf_op | source)
XLA Modules:
  0.0 113.3 jit_solution(10997312483477443642)
XLA Ops:
  0.0 112.3 %shard_map.64 = bf16[128,4096]{1,0:T(8,128)(2,1)S(1)} custom-call(bf16[128,4096]{1,0:T(8,128)(2,1)} %tok.1, s32[1,128]{1,0:T(1,128)} %bitcast.4, s32[1,128]{1,0:T(1,128)} %bitcast.5, bf16[8,4096]{1,0:T(8,128)(2,1)} %bitcast.3, bf16[1,4096,1280]{2,1,0:T(8,128)(2,1)} %w_in.1, bf16[1,1280,4096]{2,1,0:T(8,128)(2,1)} %w_out.1), custom_call_target="tpu_custom_call" | custom-call | flops 13421772800 | bytes 20971520 | tf_op jit(solution)/shard_map/pallas_call | solution.py:511
  112.3 1.0 copy.8

commit v4 on v3

--- a/solution.py
+++ b/solution.py
@@ -326,7 +326,7 @@
         second = pl.multiple_of(base + (V + v) * B, 16)
         return [ref[u, pl.ds(first, B)], ref[u, pl.ds(second, B)]]
 
-    @pl.loop(0, G + 3)
+    @pl.loop(0, G + 4)
     def _(c):
         @pl.when(c + 2 < G)
         def _():
@@ -359,32 +359,32 @@
         def _():
             gather_relay(far_g, c - 2)
 
-        @pl.when(c == 2)
+        @pl.when(c == 3)
         def _():
             for u in range(U):
                 gather_rest(near_g, u)
 
-        @pl.when(c == G + 1)
+        @pl.when(c == G + 2)
         def _():
             scatter_own(near_s, 0)
 
-        @pl.when((c >= 3) & (c < 3 + G // 2))
+        @pl.when((c >= 4) & (c < 4 + G // 2))
         def _():
             for i in range(2):
-                near_inward(2 * (c - 3) + i)
-
-        @pl.when(c == 3 + G // 2)
+                near_inward(2 * (c - 4) + i)
+
+        @pl.when(c == 4 + G // 2)
         def _():
             activate(near_acc, near_hid)
 
-        @pl.when((c >= 3 + G // 2) & (c < 3 + G // 2 + V // 2))
+        @pl.when((c >= 4 + G // 2) & (c < 4 + G // 2 + V // 2))
         def _():
             for i in range(2):
-                near_outward(2 * (c - 3 - G // 2) + i)
-
-        @pl.when(c >= 3)
-        def _():
-            k = c - 3
+                near_outward(2 * (c - 4 - G // 2) + i)
+
+        @pl.when(c >= 4)
+        def _():
+            k = c - 4
             gather_rest(far_g, k)
             widen([far_x[k, s * FAR : (s + 1) * FAR] for s in range(4)], far_p, far_chunk, FP)
             inward(far_acc, far_chunk, k)
@@ -424,7 +424,7 @@
             columns = pl.ds(pl.multiple_of(c * W + q * S, S), S)
             comb[:, columns] = term[q * T : (q + 1) * T]
 
-    @pl.loop(0, G + 4)
+    @pl.loop(0, G + 5)
     def _(c):
         @pl.when(c < G)
         def _():
@@ -450,21 +450,21 @@
         def _():
             near_outward(V + c)
 
-        @pl.when(c == 2)
+        @pl.when(c == 3)
         def _():
             near_total(0)
 
-        @pl.when((c >= 3) & (c < G + 3))
-        def _():
-            far_total(c - 3)
-
-        @pl.when(c == G + 3)
+        @pl.when((c >= 4) & (c < G + 4))
+        def _():
+            far_total(c - 4)
+
+        @pl.when(c == G + 4)
         def _():
             near_total(1)
 
-        @pl.when(c >= 4)
-        def _():
-            far_combine(c - 4)
+        @pl.when(c >= 5)
+        def _():
+            far_combine(c - 5)
 
         @pl.when(c == G)
         def _():

time: 113 us -> 111 us (0.982)
  Pallas kernels: 112 us -> 109 us
    pallas_call x1, Pallas kernels: 112 us -> 109 us  [fused(): pl.pallas_call(functools.partial(kernel, dims), out_shape=pltpu.VMEM((T,...]
where the time goes in v4:
time: 111 us; the launch traced here: 110 us
  Pallas kernels  109 us (98%)
    pallas_call x1, Pallas kernels, fused(): pl.pallas_call(functools.partial(kernel, dims), out_shape=pltpu.VMEM((T,...  109 us

profile of v4, /device:TPU:0, one launch (start us, length us, event | category | flops | bytes accessed | tf_op | source)
XLA Modules:
  0.0 110.3 jit_solution(11791733054996096798)
XLA Ops:
  0.0 109.3 %shard_map.64 = bf16[128,4096]{1,0:T(8,128)(2,1)S(1)} custom-call(bf16[128,4096]{1,0:T(8,128)(2,1)} %tok.1, s32[1,128]{1,0:T(1,128)} %bitcast.4, s32[1,128]{1,0:T(1,128)} %bitcast.5, bf16[8,4096]{1,0:T(8,128)(2,1)} %bitcast.3, bf16[1,4096,1280]{2,1,0:T(8,128)(2,1)} %w_in.1, bf16[1,1280,4096]{2,1,0:T(8,128)(2,1)} %w_out.1), custom_call_target="tpu_custom_call" | custom-call | flops 13421772800 | bytes 20971520 | tf_op jit(solution)/shard_map/pallas_call | solution.py:511
  109.3 1.0 copy.8

commit v5 on v4

--- a/solution.py
+++ b/solution.py
@@ -68,12 +68,13 @@
 
 
 def kernel(
-    dims, tok, eid, sid, router, w_in, w_out, out,
+    dims, tok_hbm, eid_hbm, sid_hbm, router_hbm, w_in, w_out, out,
+    tok, eid, sid, router,
     near_disp, far_disp, near_x, far_x, near_chunk, far_chunk, near_acc, far_acc, near_hid, far_hid, win, wout,
     near_part, far_part, near_half, far_half, near_fin, far_fin,
     near_back, far_back, near_ret, far_ret,
     d_mat, near_p, far_p, near_pt, far_pt, c_mat, gate, comb,
-    win_sem, wout_sem,
+    win_sem, wout_sem, load_sem, tok_sem,
     near_d_send, near_d_recv, far_d_send, far_d_recv,
     near_g_send, near_g_recv, far_g_send, far_g_recv,
     near_s_send, near_s_recv, far_s_send, far_s_recv,
@@ -149,6 +150,24 @@
         )[index]
         return hop(held, src_row, held, dst_row, rows, send, recv, index, c, target)
 
+    def near_hop(index, u):
+        own = pl.multiple_of(core * (V * B), 16)
+        other = pl.multiple_of((1 - core) * (V * B), 16)
+        src, src_row, target, base = (
+            (near_disp, own, xn, NEAR),
+            (near_disp, own, yn, 2 * NEAR),
+            (near_x, other, xn, NEAR),
+            (near_x, other, yn, 2 * NEAR),
+            (near_x, NEAR, yn, 3 * NEAR),
+            (near_x, 2 * NEAR + V * B, xn, 3 * NEAR + V * B),
+        )[index]
+        dst_row = base if index >= 4 else base + src_row
+        if index < 4:
+            dst_row = pl.multiple_of(dst_row, 16)
+        return hop(
+            src, src_row, near_x, dst_row, V * B, near_g_send, near_g_recv, index, u, target
+        )
+
     def scatter_hop(buffers, index, c):
         part, half, fin, n, send, recv = buffers
         h = n // 2
@@ -162,7 +181,6 @@
         )[index]
         return hop(part, src_row, dst, dst_row, h, send, recv, index, c, target)
 
-    near_g = (near_x, NEAR, near_g_send, near_g_recv)
     far_g = (far_x, FAR, far_g_send, far_g_recv)
     near_s = (near_part, near_half, near_fin, NEAR, near_s_send, near_s_recv)
     far_s = (far_part, far_half, far_fin, FAR, far_s_send, far_s_recv)
@@ -207,6 +225,20 @@
     for target in [target for target, _ in far] + [sibling, xn, yn]:
         pl.semaphore_signal(barrier, inc=1, device_id=target, device_id_type=MESH)
 
+    loads = [
+        pltpu.make_async_copy(src, dst, load_sem.at[i])
+        for i, (src, dst) in enumerate(((eid_hbm, eid), (sid_hbm, sid), (router_hbm, router)))
+    ]
+    halves = [slice(u * V * W, (u + 1) * V * W) for u in range(U)]
+    tok_loads = [
+        pltpu.make_async_copy(tok_hbm.at[:, part], tok.at[:, part], tok_sem.at[u])
+        for u, part in enumerate(halves)
+    ]
+    for copy in loads[0:2] + tok_loads + loads[2:]:
+        copy.start()
+    loads[0].wait()
+    loads[1].wait()
+
     def keys(shape, dim, first, stride):
         r = iota(shape, dim)
         block = divide(r, B)
@@ -237,20 +269,27 @@
         far_start(far_disp, far_x, far_d_send, far_d_recv, c)
 
     def near_dispatch(u):
+        tok_loads[u].wait()
         for v in range(V):
             rows = dot(d_mat[0 : 2 * B], stacked(u * V + v)).astype(BF16)
             near_disp[u, v * B : (v + 1) * B] = rows[0:B]
             near_disp[u, (V + v) * B : (V + v + 1) * B] = rows[B : 2 * B]
 
+    def near_begin(u):
+        near_start(near_disp, near_x, near_d_send, near_d_recv, u)
+        near_hop(0, u).start()
+        near_hop(1, u).start()
+
     near_dispatch(0)
     pl.semaphore_wait(barrier, E + 1)
-    near_start(near_disp, near_x, near_d_send, near_d_recv, 0)
+    near_begin(0)
     for u in range(1, U):
         near_dispatch(u)
-        near_start(near_disp, near_x, near_d_send, near_d_recv, u)
+        near_begin(u)
     for u in range(U):
         await_rows(near_x, near_d_recv, u, NEAR)
-        gather_own(near_g, u)
+        near_hop(2, u).start()
+        near_hop(3, u).start()
         far_dispatch(u)
 
     @pl.loop(0, G)
@@ -340,7 +379,12 @@
 
         @pl.when(c < U)
         def _():
-            gather_relay(near_g, c)
+            near_hop(0, c).wait_recv()
+            near_hop(2, c).wait_recv()
+            near_hop(4, c).start()
+            near_hop(1, c).wait_recv()
+            near_hop(3, c).wait_recv()
+            near_hop(5, c).start()
 
         @pl.when(c == 0)
         def _():
@@ -348,6 +392,7 @@
             cell_column = column(cell_row)
             for q in range(Q):
                 c_mat[q * T : (q + 1) * T] = one_where(key == cell_column + q * R)
+            loads[2].wait()
             logits = lax.dot_general(
                 tok[...], router[...], (((1,), (1,)), ((), ())), preferred_element_type=F32
             )
@@ -362,11 +407,8 @@
         @pl.when(c == 3)
         def _():
             for u in range(U):
-                gather_rest(near_g, u)
-
-        @pl.when(c == G + 2)
-        def _():
-            scatter_own(near_s, 0)
+                near_hop(4, u).wait_recv()
+                near_hop(5, u).wait_recv()
 
         @pl.when((c >= 4) & (c < 4 + G // 2))
         def _():
@@ -381,6 +423,10 @@
         def _():
             for i in range(2):
                 near_outward(2 * (c - 4 - G // 2) + i)
+
+        @pl.when(c == 3 + G // 2 + V // 2)
+        def _():
+            scatter_own(near_s, 0)
 
         @pl.when(c >= 4)
         def _():
@@ -424,52 +470,50 @@
             columns = pl.ds(pl.multiple_of(c * W + q * S, S), S)
             comb[:, columns] = term[q * T : (q + 1) * T]
 
-    @pl.loop(0, G + 5)
+    @pl.loop(0, G + 3)
     def _(c):
         @pl.when(c < G)
         def _():
             far_own(c)
 
+        @pl.when(c == 0)
+        def _():
+            scatter_relay(near_s, 0)
+
+        @pl.when((c >= 1) & (c <= G))
+        def _():
+            scatter_relay(far_s, c - 1)
+
         @pl.when(c == G)
         def _():
             scatter_own(near_s, 1)
 
-        @pl.when(c == 0)
-        def _():
-            scatter_relay(near_s, 0)
-
-        @pl.when((c >= 2) & (c < G + 2))
-        def _():
-            scatter_relay(far_s, c - 2)
+        @pl.when(c < G - V)
+        def _():
+            near_outward(V + c)
+
+        @pl.when(c == 2)
+        def _():
+            near_total(0)
+
+        @pl.when(c >= 3)
+        def _():
+            far_total(c - 3)
 
         @pl.when(c == G + 2)
         def _():
             scatter_relay(near_s, 1)
 
-        @pl.when(c < G - V)
-        def _():
-            near_outward(V + c)
-
-        @pl.when(c == 3)
-        def _():
-            near_total(0)
-
-        @pl.when((c >= 4) & (c < G + 4))
-        def _():
-            far_total(c - 4)
-
-        @pl.when(c == G + 4)
-        def _():
-            near_total(1)
-
-        @pl.when(c >= 5)
-        def _():
-            far_combine(c - 5)
+        @pl.when(c >= 4)
+        def _():
+            far_combine(c - 4)
 
         @pl.when(c == G)
         def _():
             combine_near(0)
 
+    near_total(1)
+    far_combine(G - 1)
     combine_near(1)
 
     @pl.loop(0, G)
@@ -484,9 +528,8 @@
     for u in range(U):
         await_rows(near_disp, near_d_send, u, V * B)
         await_rows(near_back, near_b_send, u, V * B)
-        for index in range(4):
-            gather_hop(near_g, index, u).wait_send()
         for index in range(6):
+            near_hop(index, u).wait_send()
             scatter_hop(near_s, index, u).wait_send()
 
 
@@ -511,9 +554,15 @@
     return pl.pallas_call(
         functools.partial(kernel, dims),
         out_shape=pltpu.VMEM((T, D), BF16),
-        in_specs=[vmem, vmem, vmem, vmem, hbm, hbm],
+        in_specs=[hbm] * 6,
         out_specs=vmem,
-        scratch_shapes=rows(NEAR, FAR)
+        scratch_shapes=[
+            pltpu.VMEM((T, D), BF16),
+            pltpu.VMEM((1, T), jnp.int32),
+            pltpu.VMEM((1, T), jnp.int32),
+            pltpu.VMEM((E, D), BF16),
+        ]
+        + rows(NEAR, FAR)
         + rows(4 * NEAR, 4 * FAR)
         + [
             pltpu.VMEM((4 * NP, W), BF16),
@@ -540,9 +589,9 @@
             pltpu.VMEM((T, 1), F32),
             pltpu.VMEM((T, D), F32),
         ]
-        + [dma((G,)), dma((G,))]
+        + [dma((G,)), dma((G,)), dma((3,)), dma((U,))]
         + [dma((n,)) for n in (U, U, G, G)]
-        + [dma((4, n)) for n in (U, U, G, G)]
+        + [dma((m, n)) for m, n in ((6, U), (6, U), (4, G), (4, G))]
         + [dma((6, n)) for n in (U, U, G, G)]
         + [dma((n,)) for n in (U, U, G, G)],
         compiler_params=pltpu.CompilerParams(

time: 111 us -> 109 us (0.982)
    pallas_call x1, Pallas kernels: 109 us -> 108 us  [fused(): pl.pallas_call(functools.partial(kernel, dims), out_shape=pltpu.VMEM((T,...]
where the time goes in v5:
time: 109 us; the launch traced here: 108 us
  Pallas kernels  108 us (99%)
    pallas_call x1, Pallas kernels, fused(): pl.pallas_call(functools.partial(kernel, dims), out_shape=pltpu.VMEM((T,...  108 us

profile of v5, /device:TPU:0, one launch (start us, length us, event | category | flops | bytes accessed | tf_op | source)
XLA Modules:
  0.0 108.5 jit_solution(9962070762469022277)
XLA Ops:
  0.0 107.5 %shard_map.64 = bf16[128,4096]{1,0:T(8,128)(2,1)S(1)} custom-call(bf16[128,4096]{1,0:T(8,128)(2,1)} %tok_hbm.1, s32[1,128]{1,0:T(1,128)} %bitcast.4, s32[1,128]{1,0:T(1,128)} %bitcast.5, bf16[8,4096]{1,0:T(8,128)(2,1)} %bitcast.3, bf16[1,4096,1280]{2,1,0:T(8,128)(2,1)} %w_in.1, bf16[1,1280,4096]{2,1,0:T(8,128)(2,1)} %w_out.1), custom_call_target="tpu_custom_call" | custom-call | flops 13421772800 | bytes 20971520 | tf_op jit(solution)/shard_map/pallas_call | solution.py:554
  107.5 1.0 copy.8

commit v6 on v5

--- a/solution.py
+++ b/solution.py
@@ -324,19 +324,19 @@
         return dot(pt[...], jnp.concatenate(rows, axis=0)).astype(BF16)
 
     def inward(acc, chunk, k):
-        @pl.loop(0, H // 256)
+        @pl.loop(0, H // 256, unroll=True)
         def _(n):
             columns = pl.ds(pl.multiple_of(n * 256, 256), 256)
             acc[:, columns] += dot(chunk[...], win[k, :, columns])
 
     def activate(acc, hid):
-        @pl.loop(0, H // 256)
+        @pl.loop(0, H // 256, unroll=True)
         def _(n):
             columns = pl.ds(pl.multiple_of(n * 256, 256), 256)
             hid[:, columns] = jnp.maximum(acc[:, columns], 0.0).astype(BF16)
 
     def outward(hid, chunk, k):
-        @pl.loop(0, W // 256)
+        @pl.loop(0, W // 256, unroll=True)
         def _(n):
             columns = pl.ds(pl.multiple_of(n * 256, 256), 256)
             chunk[:, columns] = dot(hid[...], wout[k, :, columns]).astype(BF16)

time: 109 us -> 102 us (0.936)
  Pallas kernels: 108 us -> 101 us
    pallas_call x1, Pallas kernels: 108 us -> 101 us  [fused(): pl.pallas_call(functools.partial(kernel, dims), out_shape=pltpu.VMEM((T,...]
where the time goes in v6:
time: 102 us
  Pallas kernels  101 us (99%)
    pallas_call x1, Pallas kernels, fused(): pl.pallas_call(functools.partial(kernel, dims), out_shape=pltpu.VMEM((T,...  101 us

profile of v6, /device:TPU:0, one launch (start us, length us, event | category | flops | bytes accessed | tf_op | source)
XLA Modules:
  0.0 102.3 jit_solution(6301077434075114628)
XLA Ops:
  0.0 101.3 %shard_map.64 = bf16[128,4096]{1,0:T(8,128)(2,1)S(1)} custom-call(bf16[128,4096]{1,0:T(8,128)(2,1)} %tok_hbm.1, s32[1,128]{1,0:T(1,128)} %bitcast.4, s32[1,128]{1,0:T(1,128)} %bitcast.5, bf16[8,4096]{1,0:T(8,128)(2,1)} %bitcast.3, bf16[1,4096,1280]{2,1,0:T(8,128)(2,1)} %w_in.1, bf16[1,1280,4096]{2,1,0:T(8,128)(2,1)} %w_out.1), custom_call_target="tpu_custom_call" | custom-call | flops 13421772800 | bytes 20971520 | tf_op jit(solution)/shard_map/pallas_call | solution.py:554
  101.4 1.0 copy.8
